TPU v7x, 32 devices: a whole 2x2x4 slice. The times are simulated.
32 devices in a mesh: section: 2 (over y), dp: 4 (over z), tower: 4 (over x, core).
Axes of the slice: x: 2, y: 2, z: 4, core: 2. Of those that a mesh axis runs over, the one named last changes fastest.
Arguments:
- stream: bfloat16 [2, 256, 4096], P(None, 'tower', 'dp'), may hold values from -17.5 to 17.5
- routes: int32 [2, 256, 1], P(None, 'tower'), may hold values from 0 to 3; in each aligned block of 64 rows (0 to 63, 64 to 127, ..., all dimensions but the last counted through in order) at most 32 rows name the same one
- tower_gain: float32 [2, 4, 4096], P('section', 'tower'), may hold values from 0.1 to 1.9
- qkv_weight: bfloat16 [2, 4, 4096, 4, 3, 128], P('section', 'tower', None, 'dp'), may hold values from -1 to 1
- out_weight: bfloat16 [2, 4, 4, 128, 4096], P('section', 'tower', None, None, 'dp'), may hold values from -0.25 to 0.25
Outputs:
- section_out: bfloat16 [2, 2, 256, 4096], P('section', None, 'tower', 'dp')
Inputs may be any that keep to these rules, and one draw needn't show every extreme that they name: `routes`: in each micro-batch at most 32 of the 64 rows of one tower device name the same tower group, and every draw reaches 32.
All inputs are finite; a program needn't handle non-finite values.
Results may differ from a plain program's by a relative error of at most 0.022.
Values may be sent and summed in bfloat16 or wider, within the bound.
A program may use at most 64 MiB of HBM per device.

v0:
```python
import jax
import jax.numpy as jnp
from jax import lax
from jax.sharding import PartitionSpec as P

NORM_EPSILON = 1e-05
MASKED = -1e30


def shifted(block, axis, distance):
    devices = range(lax.axis_size(axis))
    route = [(i - distance, i) for i in devices if i - distance in devices]
    return lax.ppermute(block, axis, route)


def slot_table(row_towers, towers, slot_count, first_row):
    row_count = row_towers.shape[0]
    member = (row_towers[:, None] == jnp.arange(towers, dtype=jnp.int32)[None, :]).astype(
        jnp.float32
    )
    earlier_mask = (jnp.arange(row_count)[:, None] > jnp.arange(row_count)[None, :]).astype(
        jnp.float32
    )
    counted = jnp.dot(earlier_mask, member, precision=lax.Precision.HIGHEST)
    position_in = jnp.sum(counted * member, axis=1).astype(jnp.int32)
    target = row_towers * slot_count + position_in
    places = jnp.arange(towers * slot_count, dtype=jnp.int32)
    chosen = target[:, None] == places[None, :]
    spread = chosen.astype(jnp.bfloat16)
    row_anchor = first_row + jnp.arange(row_count, dtype=jnp.int32)
    filled = jnp.any(chosen, axis=0)
    anchor = jnp.sum(jnp.where(chosen, row_anchor[:, None], 0), axis=0)
    anchor = jnp.where(filled, anchor, -1)
    return (spread, anchor)


def shards(stream, routes, tower_gain, qkv_weight, out_weight):
    micro_count, tok_rows, share_width = stream.shape
    towers = lax.axis_size("tower")
    sections = lax.axis_size("section")
    section_at = lax.axis_index("section")
    tower_at = lax.axis_index("tower")
    dp_at = lax.axis_index("dp")
    slot_count = tok_rows // 2
    routed_count = towers * slot_count
    gain_row = tower_gain[0, 0]
    model_width = gain_row.shape[0]
    in_weight = qkv_weight[0, 0].reshape(model_width, -1)
    head_size = in_weight.shape[1] // 3
    proj_weight = out_weight[0, 0].reshape(-1, share_width)
    score_scale = head_size ** (-0.5)
    beyond = towers * tok_rows

    def fold_heads(portion):
        return jnp.dot(portion, proj_weight, preferred_element_type=jnp.float32)

    def layer(layer_input, row_towers):
        spread, anchor = slot_table(row_towers, towers, slot_count, tower_at * tok_rows)
        whole = lax.all_gather(layer_input, "dp", axis=1, tiled=True)
        outbound = jnp.einsum(
            "rs,rf->sf", spread, whole, preferred_element_type=jnp.float32
        ).astype(jnp.bfloat16)
        inbound, slot_anchor = (
            lax.all_to_all(
                outbound.reshape(towers, slot_count, -1),
                "tower",
                split_axis=0,
                concat_axis=0,
                tiled=True,
            ),
            lax.all_to_all(
                anchor.reshape(towers, slot_count), "tower", split_axis=0, concat_axis=0, tiled=True
            ),
        )
        routed = inbound.reshape(routed_count, -1)
        slot_anchor = slot_anchor.reshape(-1)
        squares = jnp.sum(jnp.square(routed.astype(jnp.float32)), axis=1)
        scaled = (routed.astype(jnp.float32) * gain_row).astype(jnp.bfloat16)
        mixed = jnp.dot(scaled, in_weight, preferred_element_type=jnp.float32)
        own_share = lax.dynamic_slice_in_dim(routed, dp_at * share_width, share_width, 1)
        mixed = mixed * lax.rsqrt(squares / model_width + NORM_EPSILON)[:, None]
        queries = mixed[:, :head_size].astype(jnp.bfloat16)
        key_rows = mixed[:, head_size : 2 * head_size].astype(jnp.bfloat16)
        value_rows = mixed[:, 2 * head_size :].astype(jnp.bfloat16)
        query_place = jnp.where(slot_anchor < 0, beyond, slot_anchor)
        running_max = jnp.full((routed_count,), MASKED, jnp.float32)
        denominator = jnp.zeros((routed_count,), jnp.float32)
        summed = jnp.zeros((routed_count, head_size), jnp.float32)
        key_part = lax.all_gather(key_rows, "tower", axis=0, tiled=True)
        value_part = lax.all_gather(value_rows, "tower", axis=0, tiled=True)
        place_part = lax.all_gather(slot_anchor, "tower", axis=0, tiled=True)
        place_part = place_part.astype(jnp.int32)
        scores = (
            jnp.einsum("qd,kd->qk", queries, key_part, preferred_element_type=jnp.float32)
            * score_scale
        )
        visible = (place_part[None, :] >= 0) & (place_part[None, :] <= query_place[:, None])
        scores = jnp.where(visible, scores, MASKED)
        block_max = jnp.max(scores, axis=1, initial=MASKED)
        new_max = jnp.maximum(running_max, block_max)
        weights = jnp.where(visible, jnp.exp(scores - new_max[:, None]), 0.0)
        rescale = jnp.where(running_max > 0.5 * MASKED, jnp.exp(running_max - new_max), 0.0)
        denominator = denominator * rescale + jnp.sum(weights, axis=1)
        summed = summed * rescale[:, None] + jnp.dot(
            weights.astype(jnp.bfloat16), value_part, preferred_element_type=jnp.float32
        )
        running_max, denominator, summed = (new_max, denominator, summed)
        safe_total = jnp.where(denominator > 0.0, denominator, 1.0)
        attended = (summed / safe_total[:, None]).astype(jnp.bfloat16)
        projected = fold_heads(lax.all_gather(attended, "dp", axis=1, tiled=True))
        updated = (own_share.astype(jnp.float32) + projected).astype(jnp.bfloat16)
        returned = lax.all_to_all(
            updated.reshape(towers, slot_count, share_width),
            "tower",
            split_axis=0,
            concat_axis=0,
            tiled=True,
        )
        return jnp.dot(
            spread, returned.reshape(routed_count, share_width), preferred_element_type=jnp.float32
        ).astype(jnp.bfloat16)

    def advance(running, turn_at):
        incoming, stored = running
        micro_at = turn_at - section_at
        active = (micro_at >= 0) & (micro_at < micro_count)
        chosen_micro = jnp.clip(micro_at, 0, micro_count - 1)
        start_rows = lax.dynamic_index_in_dim(stream, chosen_micro, 0, keepdims=False)
        layer_input = jnp.where(section_at == 0, start_rows, incoming)
        row_towers = lax.dynamic_index_in_dim(routes, chosen_micro, 0, keepdims=False)[:, 0]
        produced = layer(layer_input, row_towers)
        produced = jnp.where(active, produced, jnp.zeros_like(produced))
        stored = jnp.where(
            active, lax.dynamic_update_index_in_dim(stored, produced, chosen_micro, 0), stored
        )
        passed = shifted(produced, "section", 1)
        return ((passed, stored), None)

    running_start = (jnp.zeros_like(stream[0]), jnp.zeros_like(stream))
    (final_pass, stored), unused = lax.scan(
        advance, running_start, jnp.arange(micro_count + sections - 1)
    )
    return stored[None]


def solution(mesh):
    placed = (
        P(None, "tower", "dp"),
        P(None, "tower", None),
        P("section", "tower", None),
        P("section", "tower", None, "dp", None, None),
        P("section", "tower", None, None, "dp"),
    )
    return jax.shard_map(
        shards,
        mesh=mesh,
        in_specs=placed,
        out_specs=P("section", None, "tower", "dp"),
        check_vma=False,
    )
```

profile of v0, /device:TPU:5, one launch (start us, length us, event | category | flops | bytes accessed | tf_op | source)
XLA Modules:
  0.0 268.6 jit_solution(3069670035273828850)
XLA Ops:
  0.0 4.8 %copy.13 = bf16[1,1,4096,1,3,128]{2,5,4,3,1,0:T(8,128)(2,1)} copy(bf16[1,1,4096,1,3,128]{5,2,4,3,1,0:T(8,128)(2,1)} %param.10) | data formatting | bytes 6291456 | tf_op args[3]
  4.8 4.8 %copy.14 = bf16[4096,384]{1,0:T(8,128)(2,1)} copy(bf16[4096,384]{0,1:T(8,128)(2,1)} %bitcast.73) | data formatting | bytes 6291456 | tf_op jit(solution)/shard_map/while | solution.py:140
  9.6 258.3 %while.15 = (s32[]{:T(128)}, bf16[64,1024]{1,0:T(8,128)(2,1)S(1)}, bf16[2,64,1024]{2,1,0:T(8,128)(2,1)S(1)}, s32[3]{0:T(128)S(1)}, s32[]{:T(128)}, /*index=5*/s3...) while((s32[]{:T(128)}, bf16[64,1024]{1,0:T(8,128)(2,1)S(1)}, ...), condition=%wide.region_7.8_spmd, body=%wide.region_0.7_spmd.sunk | while | flops 659847232 | bytes 16570499 | solution.py:140
  15.8 15.2 %all_gather.39 = bf16[64,4096]{1,0:T(8,128)(2,1)S(1)} all-gather(bf16[64,1024]{1,0:T(8,128)(2,1)S(1)} %bitcast_select_fusion.3), channel_id=1, replica_groups=mesh['section'=2,'dp'=4,'tower'=4] {'dp'}, dimensions={1}, use_global_device_ids=true | all-gather | bytes 655360 | tf_op jit(solution)/shard_map/while/body/eval_jaxpr/all_gather | solution.py:59
  32.5 4.8 %all-to-all-start = ((bf16[4,32,4096]{2,1,0:T(8,128)(2,1)}), bf16[4,32,4096]{2,1,0:T(8,128)(2,1)S(1)}, u32[]{:S(2)}, u32[]{:S(2)}) async-start(bf16[4,32,4096]{2,1,0:T(8,128)(2,1)} %bitcast.61), calls=%async_computation | async-start | bytes 2097152 | tf_op jit(solution)/shard_map/while/body/eval_jaxpr/all_to_all | solution.py:64
  38.7 13.8 %all-gather.2 = s32[4,1,128]{2,1,0:T(1,128)S(1)} all-gather(s32[1,1,128]{2,1,0:T(1,128)S(1)} %reshape.153), channel_id=1, replica_groups=mesh['section'=2,'dp'=4,'tower'=4] {'tower'}, dimensions={0}, use_global_device_ids=true | all-gather | bytes 2560 | tf_op jit(solution)/shard_map/while/body/eval_jaxpr/all_gather | solution.py:91
  55.5 5.5 %all_gather.41 = bf16[512,128]{1,0:T(8,128)(2,1)S(1)} all-gather(bf16[128,128]{1,0:T(8,128)(2,1)S(1)} %get-tuple-element.372), channel_id=1, replica_groups=mesh['section'=2,'dp'=4,'tower'=4] {'tower'}, dimensions={0}, use_global_device_ids=true | all-gather | bytes 163840 | tf_op jit(solution)/shard_map/while/body/eval_jaxpr/all_gather | solution.py:89
  61.5 5.4 %all_gather.40 = bf16[512,128]{1,0:T(8,128)(2,1)S(1)} all-gather(bf16[128,128]{1,0:T(8,128)(2,1)S(1)} %get-tuple-element.371), channel_id=1, replica_groups=mesh['section'=2,'dp'=4,'tower'=4] {'tower'}, dimensions={0}, use_global_device_ids=true | all-gather | bytes 163840 | tf_op jit(solution)/shard_map/while/body/eval_jaxpr/all_gather | solution.py:90
  67.2 10.2 %all_gather.42 = bf16[128,512]{1,0:T(8,128)(2,1)S(1)} all-gather(bf16[128,128]{1,0:T(8,128)(2,1)S(1)} %fusion.65), channel_id=1, replica_groups=mesh['section'=2,'dp'=4,'tower'=4] {'dp'}, dimensions={1}, use_global_device_ids=true | all-gather | bytes 163840 | tf_op jit(solution)/shard_map/while/body/eval_jaxpr/all_gather | solution.py:110
  78.5 5.6 %all-to-all-start.2 = ((bf16[4,32,1024]{2,1,0:T(8,128)(2,1)}), bf16[4,32,1024]{2,1,0:T(8,128)(2,1)S(1)}, u32[]{:S(2)}, u32[]{:S(2)}) async-start(bf16[4,32,1024]{2,1,0:T(8,128)(2,1)} %bitcast.67), calls=%async_computation.2 | async-start | bytes 524288 | tf_op jit(solution)/shard_map/while/body/eval_jaxpr/all_to_all | solution.py:112
  84.0 5.2 %all-to-all-done.2 = bf16[4,32,1024]{2,1,0:T(8,128)(2,1)S(1)} async-done(((bf16[4,32,1024]{2,1,0:T(8,128)(2,1)}), bf16[4,32,1024]{2,1,0:T(8,128)(2,1)S(1)}, u32[]{:S(2)}, u32[]{:S(2)}) %all-to-all-start.2) | async-done | bytes 262176 | tf_op jit(solution)/shard_map/while/body/eval_jaxpr/all_to_all | solution.py:112
  90.7 4.7 %collective-permute-done = bf16[64,1024]{1,0:T(8,128)(2,1)S(1)} collective-permute-done((bf16[64,1024]{1,0:T(8,128)(2,1)S(1)}, bf16[64,1024]{1,0:T(8,128)(2,1)S(1)}, u32[]{:S(2)}, u32[]{:S(2)}) %collective-permute-start) | collective-permute-done | bytes 131104 | tf_op jit(solution)/shard_map/while/body/eval_jaxpr/ppermute | solution.py:13
  97.8 5.0 %all-to-all-start.1 = ((s32[4,1,32]{2,1,0:T(1,128)}), s32[4,1,32]{2,1,0:T(1,128)S(1)}, u32[]{:S(2)}, u32[]{:S(2)}) async-start(s32[4,1,32]{2,1,0:T(1,128)} %bitcast.64), calls=%async_computation.1 | async-start | bytes 4096 | tf_op jit(solution)/shard_map/while/body/eval_jaxpr/all_to_all | solution.py:71
  102.7 13.8 %all_gather.39 = bf16[64,4096]{1,0:T(8,128)(2,1)S(1)} all-gather(bf16[64,1024]{1,0:T(8,128)(2,1)S(1)} %bitcast_select_fusion.3), channel_id=1, replica_groups=mesh['section'=2,'dp'=4,'tower'=4] {'dp'}, dimensions={1}, use_global_device_ids=true | all-gather | bytes 655360 | tf_op jit(solution)/shard_map/while/body/eval_jaxpr/all_gather | solution.py:59
  118.1 5.4 %all-to-all-start = ((bf16[4,32,4096]{2,1,0:T(8,128)(2,1)}), bf16[4,32,4096]{2,1,0:T(8,128)(2,1)S(1)}, u32[]{:S(2)}, u32[]{:S(2)}) async-start(bf16[4,32,4096]{2,1,0:T(8,128)(2,1)} %bitcast.61), calls=%async_computation | async-start | bytes 2097152 | tf_op jit(solution)/shard_map/while/body/eval_jaxpr/all_to_all | solution.py:64
  124.9 13.8 %all-gather.2 = s32[4,1,128]{2,1,0:T(1,128)S(1)} all-gather(s32[1,1,128]{2,1,0:T(1,128)S(1)} %reshape.153), channel_id=1, replica_groups=mesh['section'=2,'dp'=4,'tower'=4] {'tower'}, dimensions={0}, use_global_device_ids=true | all-gather | bytes 2560 | tf_op jit(solution)/shard_map/while/body/eval_jaxpr/all_gather | solution.py:91
  141.7 5.5 %all_gather.41 = bf16[512,128]{1,0:T(8,128)(2,1)S(1)} all-gather(bf16[128,128]{1,0:T(8,128)(2,1)S(1)} %get-tuple-element.372), channel_id=1, replica_groups=mesh['section'=2,'dp'=4,'tower'=4] {'tower'}, dimensions={0}, use_global_device_ids=true | all-gather | bytes 163840 | tf_op jit(solution)/shard_map/while/body/eval_jaxpr/all_gather | solution.py:89
  147.7 5.4 %all_gather.40 = bf16[512,128]{1,0:T(8,128)(2,1)S(1)} all-gather(bf16[128,128]{1,0:T(8,128)(2,1)S(1)} %get-tuple-element.371), channel_id=1, replica_groups=mesh['section'=2,'dp'=4,'tower'=4] {'tower'}, dimensions={0}, use_global_device_ids=true | all-gather | bytes 163840 | tf_op jit(solution)/shard_map/while/body/eval_jaxpr/all_gather | solution.py:90
  153.4 9.9 %all_gather.42 = bf16[128,512]{1,0:T(8,128)(2,1)S(1)} all-gather(bf16[128,128]{1,0:T(8,128)(2,1)S(1)} %fusion.65), channel_id=1, replica_groups=mesh['section'=2,'dp'=4,'tower'=4] {'dp'}, dimensions={1}, use_global_device_ids=true | all-gather | bytes 163840 | tf_op jit(solution)/shard_map/while/body/eval_jaxpr/all_gather | solution.py:110
  164.3 5.9 %all-to-all-start.2 = ((bf16[4,32,1024]{2,1,0:T(8,128)(2,1)}), bf16[4,32,1024]{2,1,0:T(8,128)(2,1)S(1)}, u32[]{:S(2)}, u32[]{:S(2)}) async-start(bf16[4,32,1024]{2,1,0:T(8,128)(2,1)} %bitcast.67), calls=%async_computation.2 | async-start | bytes 524288 | tf_op jit(solution)/shard_map/while/body/eval_jaxpr/all_to_all | solution.py:112
  170.2 5.2 %all-to-all-done.2 = bf16[4,32,1024]{2,1,0:T(8,128)(2,1)S(1)} async-done(((bf16[4,32,1024]{2,1,0:T(8,128)(2,1)}), bf16[4,32,1024]{2,1,0:T(8,128)(2,1)S(1)}, u32[]{:S(2)}, u32[]{:S(2)}) %all-to-all-start.2) | async-done | bytes 262176 | tf_op jit(solution)/shard_map/while/body/eval_jaxpr/all_to_all | solution.py:112
  176.9 4.7 %collective-permute-done = bf16[64,1024]{1,0:T(8,128)(2,1)S(1)} collective-permute-done((bf16[64,1024]{1,0:T(8,128)(2,1)S(1)}, bf16[64,1024]{1,0:T(8,128)(2,1)S(1)}, u32[]{:S(2)}, u32[]{:S(2)}) %collective-permute-start) | collective-permute-done | bytes 131104 | tf_op jit(solution)/shard_map/while/body/eval_jaxpr/ppermute | solution.py:13
  183.9 5.0 %all-to-all-start.1 = ((s32[4,1,32]{2,1,0:T(1,128)}), s32[4,1,32]{2,1,0:T(1,128)S(1)}, u32[]{:S(2)}, u32[]{:S(2)}) async-start(s32[4,1,32]{2,1,0:T(1,128)} %bitcast.64), calls=%async_computation.1 | async-start | bytes 4096 | tf_op jit(solution)/shard_map/while/body/eval_jaxpr/all_to_all | solution.py:71
  188.9 13.9 %all_gather.39 = bf16[64,4096]{1,0:T(8,128)(2,1)S(1)} all-gather(bf16[64,1024]{1,0:T(8,128)(2,1)S(1)} %bitcast_select_fusion.3), channel_id=1, replica_groups=mesh['section'=2,'dp'=4,'tower'=4] {'dp'}, dimensions={1}, use_global_device_ids=true | all-gather | bytes 655360 | tf_op jit(solution)/shard_map/while/body/eval_jaxpr/all_gather | solution.py:59
  204.3 5.5 %all-to-all-start = ((bf16[4,32,4096]{2,1,0:T(8,128)(2,1)}), bf16[4,32,4096]{2,1,0:T(8,128)(2,1)S(1)}, u32[]{:S(2)}, u32[]{:S(2)}) async-start(bf16[4,32,4096]{2,1,0:T(8,128)(2,1)} %bitcast.61), calls=%async_computation | async-start | bytes 2097152 | tf_op jit(solution)/shard_map/while/body/eval_jaxpr/all_to_all | solution.py:64
  211.2 13.8 %all-gather.2 = s32[4,1,128]{2,1,0:T(1,128)S(1)} all-gather(s32[1,1,128]{2,1,0:T(1,128)S(1)} %reshape.153), channel_id=1, replica_groups=mesh['section'=2,'dp'=4,'tower'=4] {'tower'}, dimensions={0}, use_global_device_ids=true | all-gather | bytes 2560 | tf_op jit(solution)/shard_map/while/body/eval_jaxpr/all_gather | solution.py:91
  228.0 5.5 %all_gather.41 = bf16[512,128]{1,0:T(8,128)(2,1)S(1)} all-gather(bf16[128,128]{1,0:T(8,128)(2,1)S(1)} %get-tuple-element.372), channel_id=1, replica_groups=mesh['section'=2,'dp'=4,'tower'=4] {'tower'}, dimensions={0}, use_global_device_ids=true | all-gather | bytes 163840 | tf_op jit(solution)/shard_map/while/body/eval_jaxpr/all_gather | solution.py:89
  234.0 5.4 %all_gather.40 = bf16[512,128]{1,0:T(8,128)(2,1)S(1)} all-gather(bf16[128,128]{1,0:T(8,128)(2,1)S(1)} %get-tuple-element.371), channel_id=1, replica_groups=mesh['section'=2,'dp'=4,'tower'=4] {'tower'}, dimensions={0}, use_global_device_ids=true | all-gather | bytes 163840 | tf_op jit(solution)/shard_map/while/body/eval_jaxpr/all_gather | solution.py:90
  239.7 9.9 %all_gather.42 = bf16[128,512]{1,0:T(8,128)(2,1)S(1)} all-gather(bf16[128,128]{1,0:T(8,128)(2,1)S(1)} %fusion.65), channel_id=1, replica_groups=mesh['section'=2,'dp'=4,'tower'=4] {'dp'}, dimensions={1}, use_global_device_ids=true | all-gather | bytes 163840 | tf_op jit(solution)/shard_map/while/body/eval_jaxpr/all_gather | solution.py:110
  250.6 5.9 %all-to-all-start.2 = ((bf16[4,32,1024]{2,1,0:T(8,128)(2,1)}), bf16[4,32,1024]{2,1,0:T(8,128)(2,1)S(1)}, u32[]{:S(2)}, u32[]{:S(2)}) async-start(bf16[4,32,1024]{2,1,0:T(8,128)(2,1)} %bitcast.67), calls=%async_computation.2 | async-start | bytes 524288 | tf_op jit(solution)/shard_map/while/body/eval_jaxpr/all_to_all | solution.py:112
  256.5 5.2 %all-to-all-done.2 = bf16[4,32,1024]{2,1,0:T(8,128)(2,1)S(1)} async-done(((bf16[4,32,1024]{2,1,0:T(8,128)(2,1)}), bf16[4,32,1024]{2,1,0:T(8,128)(2,1)S(1)}, u32[]{:S(2)}, u32[]{:S(2)}) %all-to-all-start.2) | async-done | bytes 262176 | tf_op jit(solution)/shard_map/while/body/eval_jaxpr/all_to_all | solution.py:112
  263.2 4.7 %collective-permute-done = bf16[64,1024]{1,0:T(8,128)(2,1)S(1)} collective-permute-done((bf16[64,1024]{1,0:T(8,128)(2,1)S(1)}, bf16[64,1024]{1,0:T(8,128)(2,1)S(1)}, u32[]{:S(2)}, u32[]{:S(2)}) %collective-permute-start) | collective-permute-done | bytes 131104 | tf_op jit(solution)/shard_map/while/body/eval_jaxpr/ppermute | solution.py:13
  (107 shorter events, 37.1 us)
Async XLA Ops:
  4.8 4.8 %copy-start = (bf16[1,1,4,128,1024]{4,3,2,1,0:T(8,128)(2,1)S(1)}, bf16[1,1,4,128,1024]{4,3,2,1,0:T(8,128)(2,1)}, u32[]{:S(2)}) copy-start(bf16[1,1,4,128,1024]{4,3,2,1,0:T(8,128)(2,1)} %param.11) | copy-start | bytes 3145732
  4.8 4.8 %copy-start.2 = (bf16[2,64,1024]{2,1,0:T(8,128)(2,1)S(1)}, bf16[2,64,1024]{2,1,0:T(8,128)(2,1)}, u32[]{:S(2)}) copy-start(bf16[2,64,1024]{2,1,0:T(8,128)(2,1)} %param.7) | copy-start | bytes 786436
  4.8 4.8 %copy-start.3 = (f32[1,1,4096]{2,1,0:T(1,128)S(1)}, f32[1,1,4096]{2,1,0:T(1,128)}, u32[]{:S(2)}) copy-start(f32[1,1,4096]{2,1,0:T(1,128)} %param.9) | copy-start | bytes 49156
  4.8 4.8 %copy-start.4 = (s32[2,64,1]{1,2,0:T(1,128)S(1)}, s32[2,64,1]{1,2,0:T(1,128)}, u32[]{:S(2)}) copy-start(s32[2,64,1]{1,2,0:T(1,128)} %param.8) | copy-start | bytes 1540
  11.9 20.6 %all-to-all-start.1 = ((s32[4,1,32]{2,1,0:T(1,128)}), s32[4,1,32]{2,1,0:T(1,128)S(1)}, u32[]{:S(2)}, u32[]{:S(2)}) async-start(s32[4,1,32]{2,1,0:T(1,128)} %bitcast.64), calls=%async_computation.1 | async-start | bytes 4096 | tf_op jit(solution)/shard_map/while/body/eval_jaxpr/all_to_all | solution.py:71
  32.5 20.0 %all-to-all-start = ((bf16[4,32,4096]{2,1,0:T(8,128)(2,1)}), bf16[4,32,4096]{2,1,0:T(8,128)(2,1)S(1)}, u32[]{:S(2)}, u32[]{:S(2)}) async-start(bf16[4,32,4096]{2,1,0:T(8,128)(2,1)} %bitcast.61), calls=%async_computation | async-start | bytes 2097152 | tf_op jit(solution)/shard_map/while/body/eval_jaxpr/all_to_all | solution.py:64
  78.5 10.7 %all-to-all-start.2 = ((bf16[4,32,1024]{2,1,0:T(8,128)(2,1)}), bf16[4,32,1024]{2,1,0:T(8,128)(2,1)S(1)}, u32[]{:S(2)}, u32[]{:S(2)}) async-start(bf16[4,32,1024]{2,1,0:T(8,128)(2,1)} %bitcast.67), calls=%async_computation.2 | async-start | bytes 524288 | tf_op jit(solution)/shard_map/while/body/eval_jaxpr/all_to_all | solution.py:112
  89.4 6.0 %collective-permute-start = (bf16[64,1024]{1,0:T(8,128)(2,1)S(1)}, bf16[64,1024]{1,0:T(8,128)(2,1)S(1)}, u32[]{:S(2)}, u32[]{:S(2)}) collective-permute-start(bf16[64,1024]{1,0:T(8,128)(2,1)S(1)} %get-tuple-element.376), channel_id=1, source_target_pairs={{0,16},{1,17},{2,18},{3,19},{4,20},{5,21},{6,22},{7,23},{8,24},{9,... | collective-permute-start | bytes 393224 | tf_op jit(solution)/shard_map/while/body/eval_jaxpr/ppermute | solution.py:13
  97.8 20.4 %all-to-all-start.1 = ((s32[4,1,32]{2,1,0:T(1,128)}), s32[4,1,32]{2,1,0:T(1,128)S(1)}, u32[]{:S(2)}, u32[]{:S(2)}) async-start(s32[4,1,32]{2,1,0:T(1,128)} %bitcast.64), calls=%async_computation.1 | async-start | bytes 4096 | tf_op jit(solution)/shard_map/while/body/eval_jaxpr/all_to_all | solution.py:71
  118.1 20.6 %all-to-all-start = ((bf16[4,32,4096]{2,1,0:T(8,128)(2,1)}), bf16[4,32,4096]{2,1,0:T(8,128)(2,1)S(1)}, u32[]{:S(2)}, u32[]{:S(2)}) async-start(bf16[4,32,4096]{2,1,0:T(8,128)(2,1)} %bitcast.61), calls=%async_computation | async-start | bytes 2097152 | tf_op jit(solution)/shard_map/while/body/eval_jaxpr/all_to_all | solution.py:64
  164.3 11.1 %all-to-all-start.2 = ((bf16[4,32,1024]{2,1,0:T(8,128)(2,1)}), bf16[4,32,1024]{2,1,0:T(8,128)(2,1)S(1)}, u32[]{:S(2)}, u32[]{:S(2)}) async-start(bf16[4,32,1024]{2,1,0:T(8,128)(2,1)} %bitcast.67), calls=%async_computation.2 | async-start | bytes 524288 | tf_op jit(solution)/shard_map/while/body/eval_jaxpr/all_to_all | solution.py:112
  175.6 6.0 %collective-permute-start = (bf16[64,1024]{1,0:T(8,128)(2,1)S(1)}, bf16[64,1024]{1,0:T(8,128)(2,1)S(1)}, u32[]{:S(2)}, u32[]{:S(2)}) collective-permute-start(bf16[64,1024]{1,0:T(8,128)(2,1)S(1)} %get-tuple-element.376), channel_id=1, source_target_pairs={{0,16},{1,17},{2,18},{3,19},{4,20},{5,21},{6,22},{7,23},{8,24},{9,... | collective-permute-start | bytes 393224 | tf_op jit(solution)/shard_map/while/body/eval_jaxpr/ppermute | solution.py:13
  183.9 20.4 %all-to-all-start.1 = ((s32[4,1,32]{2,1,0:T(1,128)}), s32[4,1,32]{2,1,0:T(1,128)S(1)}, u32[]{:S(2)}, u32[]{:S(2)}) async-start(s32[4,1,32]{2,1,0:T(1,128)} %bitcast.64), calls=%async_computation.1 | async-start | bytes 4096 | tf_op jit(solution)/shard_map/while/body/eval_jaxpr/all_to_all | solution.py:71
  204.3 20.7 %all-to-all-start = ((bf16[4,32,4096]{2,1,0:T(8,128)(2,1)}), bf16[4,32,4096]{2,1,0:T(8,128)(2,1)S(1)}, u32[]{:S(2)}, u32[]{:S(2)}) async-start(bf16[4,32,4096]{2,1,0:T(8,128)(2,1)} %bitcast.61), calls=%async_computation | async-start | bytes 2097152 | tf_op jit(solution)/shard_map/while/body/eval_jaxpr/all_to_all | solution.py:64
  250.6 11.1 %all-to-all-start.2 = ((bf16[4,32,1024]{2,1,0:T(8,128)(2,1)}), bf16[4,32,1024]{2,1,0:T(8,128)(2,1)S(1)}, u32[]{:S(2)}, u32[]{:S(2)}) async-start(bf16[4,32,1024]{2,1,0:T(8,128)(2,1)} %bitcast.67), calls=%async_computation.2 | async-start | bytes 524288 | tf_op jit(solution)/shard_map/while/body/eval_jaxpr/all_to_all | solution.py:112
  261.9 6.0 %collective-permute-start = (bf16[64,1024]{1,0:T(8,128)(2,1)S(1)}, bf16[64,1024]{1,0:T(8,128)(2,1)S(1)}, u32[]{:S(2)}, u32[]{:S(2)}) collective-permute-start(bf16[64,1024]{1,0:T(8,128)(2,1)S(1)} %get-tuple-element.376), channel_id=1, source_target_pairs={{0,16},{1,17},{2,18},{3,19},{4,20},{5,21},{6,22},{7,23},{8,24},{9,... | collective-permute-start | bytes 393224 | tf_op jit(solution)/shard_map/while/body/eval_jaxpr/ppermute | solution.py:13
  267.9 0.7 copy-start.1
where the time goes:
time: 271 us; the launch traced here: 269 us
  blocking collectives  147 us (54%)
  starting transfers between devices  50.7 us (19%)
  waiting for transfers between devices  29.7 us (11%)
  matrix products  18.2 us (7%)
  local copies, waits for them, and re-layouts  16.3 us (6%)
  other arithmetic  4.35 us (2%)
    all_gather x3, blocking collectives, layer(): whole = lax.all_gather(layer_input, 'dp', axis=1, tiled=True)  42.9 us
    all_gather x3, blocking collectives, layer(): place_part = lax.all_gather(slot_anchor, 'tower', axis=0, tiled=True)  41.4 us
    all_gather x3, blocking collectives, layer(): projected = fold_heads(lax.all_gather(attended, 'dp', axis=1, tiled=True))  30.1 us
    all_to_all x3, starting transfers between devices, layer(): lax.all_to_all(updated.reshape(towers, slot_count, share_width), 'tower',...  17.3 us
    all_gather x3, blocking collectives, layer(): key_part = lax.all_gather(key_rows, 'tower', axis=0, tiled=True)  16.4 us
    all_gather x3, blocking collectives, layer(): value_part = lax.all_gather(value_rows, 'tower', axis=0, tiled=True)  16.3 us
    all_to_all x3, starting transfers between devices, layer(): lax.all_to_all(outbound.reshape(towers, slot_count, -1), 'tower', split_a...  15.7 us
    all_to_all x3, waiting for transfers between devices, layer(): lax.all_to_all(updated.reshape(towers, slot_count, share_width), 'tower',...  15.5 us
  transfers between devices with their start and end apart: 12, of which 6 were waited for; matrix products, arithmetic and copies ran while one was open for 3% of the time, Pallas kernels for 0%

commit v1 on v0

v1 whole, which is shorter than its diff:
```python
import functools

import jax
import jax.numpy as jnp
from jax import lax
from jax.experimental import pallas as pl
from jax.experimental.pallas import tpu as pltpu
from jax.sharding import PartitionSpec as P

NORM_EPSILON = 1e-05
MASKED = -1e30
MESH = pl.DeviceIdType.MESH


def unslot(spread, slots):
    return lax.dot_general(
        spread, slots, (((0,), (0,)), ((), ())), preferred_element_type=jnp.float32
    )


def kernel(
    sections, dps, towers,
    stream, routes, gain, qkv_hbm, out_hbm, out,
    w_in, w_out, routes_of, spread_of, rows_in, shares, outbound, inbound,
    queries, kv_out, kv_all, heads, updated, returned,
    w_sem, r_send, r_recv, z_send, z_recv, x_send, x_recv, kv_send, kv_recv,
    a_send, a_recv, b_send, b_recv, s_send, s_recv,
):
    micros, rows, width = stream.shape
    slots = rows // 2
    routed = towers * slots
    head = qkv_hbm.shape[2]
    section_at = lax.axis_index("section")
    dp_at = lax.axis_index("dp")
    tower_at = lax.axis_index("tower")
    next_section = lax.rem(section_at + 1, sections)
    prev_section = lax.rem(section_at + sections - 1, sections)

    def ahead(me, k, n):
        return lax.rem(me + k, n)

    weight_copies = [
        pltpu.make_async_copy(
            qkv_hbm.at[j], w_in.at[:, pl.ds(j * head, head)], w_sem.at[j]
        )
        for j in range(3)
    ]
    weight_copies.append(pltpu.make_async_copy(out_hbm, w_out, w_sem.at[3]))
    for copy in weight_copies:
        copy.start()

    barrier = pltpu.get_barrier_semaphore()
    for k in range(1, dps):
        pl.semaphore_signal(
            barrier, inc=1, device_id={"dp": ahead(dp_at, k, dps)}, device_id_type=MESH
        )
    for k in range(1, towers):
        pl.semaphore_signal(
            barrier, inc=1, device_id={"tower": ahead(tower_at, k, towers)}, device_id_type=MESH
        )

    @pl.when(section_at > 0)
    def _():
        pl.semaphore_signal(
            barrier, inc=1, device_id={"section": prev_section}, device_id_type=MESH
        )

    for m in range(micros):
        routes_of[tower_at, m : m + 1, 0:rows] = routes[m]

    @pl.when(section_at < sections - 1)
    def _():
        pl.semaphore_wait(barrier, dps + towers - 1)

    @pl.when(section_at == sections - 1)
    def _():
        pl.semaphore_wait(barrier, dps + towers - 2)

    started = []

    def send(src, dst, send_sem, recv_sem, device_id):
        copy = pltpu.make_async_remote_copy(
            src_ref=src, dst_ref=dst, send_sem=send_sem, recv_sem=recv_sem,
            device_id=device_id, device_id_type=MESH,
        )
        copy.start()
        started.append(copy)
        return copy

    route_copies = [
        send(
            routes_of.at[tower_at], routes_of.at[tower_at], r_send.at[k], r_recv.at[k],
            {"tower": ahead(tower_at, k, towers)},
        )
        for k in range(1, towers)
    ]

    lane = lax.broadcasted_iota(jnp.int32, (rows, rows), 1)
    sublane = lax.broadcasted_iota(jnp.int32, (rows, rows), 0)
    earlier = (sublane < lane).astype(jnp.bfloat16)
    tower_iota = lax.broadcasted_iota(jnp.int32, (16, rows), 0)
    slot_iota = lax.broadcasted_iota(jnp.int32, (slots, rows), 0).astype(jnp.float32)

    def make_spread(m, block):
        named = routes_of[block, m : m + 1, 0:rows]
        member = (jnp.broadcast_to(named, (16, rows)) == tower_iota).astype(jnp.float32)
        counted = jnp.dot(
            member.astype(jnp.bfloat16), earlier, preferred_element_type=jnp.float32
        )
        place = jnp.where(member > 0.0, counted, -1.0)
        for t in range(towers):
            hit = jnp.broadcast_to(place[t : t + 1], (slots, rows)) == slot_iota
            spread_of[m, block, t] = hit.astype(jnp.float32).astype(jnp.bfloat16)

    relays = [
        pltpu.make_async_remote_copy(
            src_ref=out.at[0, m], dst_ref=rows_in.at[m], send_sem=s_send.at[m],
            recv_sem=s_recv.at[m], device_id={"section": next_section}, device_id_type=MESH,
        )
        for m in range(micros)
    ]
    z_copies, x_copies, kv_copies, a_copies, b_copies = {}, {}, {}, {}, {}

    def enter(m):
        @pl.when(section_at == 0)
        def _():
            rows_in[m] = stream[m]

        @pl.when(section_at > 0)
        def _():
            relays[m].wait_recv()

        for k in range(1, dps):
            z_copies[m, k] = send(
                rows_in.at[m], shares.at[m, k], z_send.at[m, k], z_recv.at[m, k],
                {"dp": ahead(dp_at, k, dps)},
            )

    def route(m, k):
        if k == 0:
            share = rows_in[m]
        else:
            z_copies[m, k].wait_recv()
            share = shares[m, k]
        spread = spread_of[m, tower_at].reshape(routed, rows)
        picked = jnp.dot(spread, share, preferred_element_type=jnp.float32)
        outbound[m, k] = picked.astype(jnp.bfloat16).reshape(towers, slots, width)
        for j in range(1, towers):
            peer = ahead(tower_at, j, towers)
            x_copies[m, k, j] = send(
                outbound.at[m, k, peer], inbound.at[m, k, tower_at],
                x_send.at[m, k, j], x_recv.at[m, k, j], {"tower": peer},
            )
        inbound[m, k, tower_at] = outbound[m, k, tower_at]

    def project_in(m):
        total = jnp.zeros((routed, 3 * head), jnp.float32)
        squares = jnp.zeros((routed, 1), jnp.float32)
        for k in range(dps):
            for j in range(1, towers):
                x_copies[m, k, j].wait_recv()
            owner = lax.rem(dp_at + dps - k, dps)
            at = pl.ds(pl.multiple_of(owner * width, width), width)
            value = inbound[m, k].reshape(routed, width).astype(jnp.float32)
            squares = squares + jnp.sum(value * value, axis=1, keepdims=True)
            scaled = (value * gain[:, at]).astype(jnp.bfloat16)
            total = total + jnp.dot(scaled, w_in[at, :], preferred_element_type=jnp.float32)
        mixed = total * lax.rsqrt(squares / (width * dps) + NORM_EPSILON)
        queries[m] = mixed[:, :head].astype(jnp.bfloat16)
        kv_out[m] = mixed[:, head:].astype(jnp.bfloat16).reshape(towers, slots, 2 * head)
        for j in range(1, towers):
            kv_copies[m, j] = send(
                kv_out.at[m], kv_all.at[m, :, tower_at], kv_send.at[m, j], kv_recv.at[m, j],
                {"tower": ahead(tower_at, j, towers)},
            )
        for block in range(towers):
            kv_all[m, block, tower_at] = kv_out[m, block]

    def attend(m):
        place_iota = lax.broadcasted_iota(jnp.int32, (slots, rows), 1).astype(jnp.float32)
        anchors = jnp.concatenate(
            [
                jnp.sum(
                    spread_of[m, block, tower_at].astype(jnp.float32)
                    * (place_iota + float(block * rows)),
                    axis=1, keepdims=True,
                )
                for block in range(towers)
            ],
            axis=0,
        )
        for j in range(1, towers):
            kv_copies[m, j].wait_recv()
        kv = jnp.concatenate(
            [
                unslot(
                    spread_of[m, block].reshape(routed, rows),
                    kv_all[m, block].reshape(routed, 2 * head),
                ).astype(jnp.bfloat16)
                for block in range(towers)
            ],
            axis=0,
        )
        scores = lax.dot_general(
            queries[m], kv[:, :head], (((1,), (1,)), ((), ())),
            preferred_element_type=jnp.float32,
        ) * (head ** -0.5)
        column = lax.broadcasted_iota(jnp.int32, scores.shape, 1).astype(jnp.float32)
        visible = column <= anchors
        scores = jnp.where(visible, scores, MASKED)
        highest = jnp.max(scores, axis=1, keepdims=True)
        weights = jnp.where(visible, jnp.exp(scores - highest), 0.0)
        denominator = jnp.sum(weights, axis=1, keepdims=True)
        summed = jnp.dot(
            weights.astype(jnp.bfloat16), kv[:, head:], preferred_element_type=jnp.float32
        )
        own = pl.ds(pl.multiple_of(dp_at * head, head), head)
        heads[m, :, own] = (summed / denominator).astype(jnp.bfloat16)
        for k in range(1, dps):
            a_copies[m, k] = send(
                heads.at[m, :, own], heads.at[m, :, own], a_send.at[m, k], a_recv.at[m, k],
                {"dp": ahead(dp_at, k, dps)},
            )

    def project_out(m):
        for k in range(1, dps):
            a_copies[m, k].wait_recv()
        made = jnp.dot(heads[m], w_out[...], preferred_element_type=jnp.float32)
        own = inbound[m, 0].reshape(routed, width).astype(jnp.float32)
        updated[m] = (own + made).astype(jnp.bfloat16).reshape(towers, slots, width)
        for j in range(1, towers):
            peer = ahead(tower_at, j, towers)
            b_copies[m, j] = send(
                updated.at[m, peer], returned.at[m, tower_at], b_send.at[m, j], b_recv.at[m, j],
                {"tower": peer},
            )
        returned[m, tower_at] = updated[m, tower_at]

    def leave(m):
        for j in range(1, towers):
            b_copies[m, j].wait_recv()
        spread = spread_of[m, tower_at].reshape(routed, rows)
        out[0, m] = unslot(spread, returned[m].reshape(routed, width)).astype(jnp.bfloat16)

        @pl.when(section_at < sections - 1)
        def _():
            relays[m].start()

    for m in range(micros):
        make_spread(m, tower_at)
    enter(0)
    for k in range(dps):
        route(0, k)
    for k in range(1, towers):
        route_copies[k - 1].wait_recv()
        for m in range(micros):
            make_spread(m, lax.rem(tower_at + towers - k, towers))
    for copy in weight_copies:
        copy.wait()

    later = [project_in, attend, project_out, leave]
    for m in range(micros):
        pending = list(range(dps)) if m + 1 < micros else []
        if pending:
            enter(m + 1)
            route(m + 1, pending.pop(0))
        for number, step in enumerate(later):
            step(m)
            left = len(later) - 1 - number
            if pending and left:
                for k in range(-(-len(pending) // left)):
                    route(m + 1, pending.pop(0))

    for copy in started:
        copy.wait_send()

    @pl.when(section_at < sections - 1)
    def _():
        for m in range(micros):
            relays[m].wait_send()


def shards(stream, routes, tower_gain, qkv_weight, out_weight):
    micros, rows, width = stream.shape
    sections = lax.axis_size("section")
    dps = lax.axis_size("dp")
    towers = lax.axis_size("tower")
    head = qkv_weight.shape[-1]
    model = tower_gain.shape[-1]
    slots = rows // 2
    routed = towers * slots
    bf16 = jnp.bfloat16
    dma = pltpu.SemaphoreType.DMA
    vmem = pl.BlockSpec(memory_space=pltpu.VMEM)
    hbm = pl.BlockSpec(memory_space=pl.ANY)
    return pl.pallas_call(
        functools.partial(kernel, sections, dps, towers),
        out_shape=jax.ShapeDtypeStruct((1, micros, rows, width), bf16),
        in_specs=[vmem, vmem, vmem, hbm, hbm],
        out_specs=vmem,
        scratch_shapes=[
            pltpu.VMEM((model, 3 * head), bf16),
            pltpu.VMEM((dps * head, width), bf16),
            pltpu.VMEM((towers, 8, 128), jnp.int32),
            pltpu.VMEM((micros, towers, towers, slots, rows), bf16),
            pltpu.VMEM((micros, rows, width), bf16),
            pltpu.VMEM((micros, dps, rows, width), bf16),
            pltpu.VMEM((micros, dps, towers, slots, width), bf16),
            pltpu.VMEM((micros, dps, towers, slots, width), bf16),
            pltpu.VMEM((micros, routed, head), bf16),
            pltpu.VMEM((micros, towers, slots, 2 * head), bf16),
            pltpu.VMEM((micros, towers, towers, slots, 2 * head), bf16),
            pltpu.VMEM((micros, routed, dps * head), bf16),
            pltpu.VMEM((micros, towers, slots, width), bf16),
            pltpu.VMEM((micros, towers, slots, width), bf16),
            dma((4,)),
            dma((towers,)), dma((towers,)),
            dma((micros, dps)), dma((micros, dps)),
            dma((micros, dps, towers)), dma((micros, dps, towers)),
            dma((micros, towers)), dma((micros, towers)),
            dma((micros, dps)), dma((micros, dps)),
            dma((micros, towers)), dma((micros, towers)),
            dma((micros,)), dma((micros,)),
        ],
        compiler_params=pltpu.CompilerParams(
            collective_id=0, has_side_effects=True, vmem_limit_bytes=48 * 1024 * 1024
        ),
        name="relay",
    )(
        stream,
        jnp.transpose(routes, (0, 2, 1)),
        tower_gain.reshape(1, model),
        jnp.transpose(qkv_weight.reshape(model, 3, head), (1, 0, 2)),
        out_weight.reshape(dps * head, width),
    )


def solution(mesh):
    placed = (
        P(None, "tower", "dp"),
        P(None, "tower", None),
        P("section", "tower", None),
        P("section", "tower", None, "dp", None, None),
        P("section", "tower", None, None, "dp"),
    )
    return jax.shard_map(
        shards,
        mesh=mesh,
        in_specs=placed,
        out_specs=P("section", None, "tower", "dp"),
        check_vma=False,
    )
```

time: 271 us -> 107 us (0.39)
  blocking collectives: 147 us -> 0 us
  Pallas kernels: 0 us -> 100 us
  starting transfers between devices: 50.7 us -> 0 us
  waiting for transfers between devices: 29.7 us -> 0 us
  matrix products: 18.2 us -> 0 us
  local copies, waits for them, and re-layouts: 16.3 us -> 6.16 us
  other arithmetic: 4.35 us -> 0 us
    all_gather x15 -> x0, blocking collectives: 147 us -> none  [the longest x3 42.9 us: layer(): whole = lax.all_gather(layer_input, 'dp', axis=1, tiled=True)]
    pallas_call x0 -> x1, Pallas kernels: none -> 100 us  [shards(): pl.pallas_call(functools.partial(kernel, sections, dps, towers), out_shap...]
    all_to_all x9 -> x0, starting transfers between devices: 46.8 us -> none  [the longest x3 17.3 us: layer(): lax.all_to_all(updated.reshape(towers, slot_count, share_width), 'tower',...]
    dot_general x21 -> x0, matrix products: 18.2 us -> none  [the longest x3 7.81 us: layer(): mixed = jnp.dot(scaled, in_weight, preferred_element_type=jnp.float32)]
    all_to_all x9 -> x0, waiting for transfers between devices: 15.5 us -> none  [the longest x3 15.5 us: layer(): lax.all_to_all(updated.reshape(towers, slot_count, share_width), 'tower',...]
    ppermute x3 -> x0, waiting for transfers between devices: 14.2 us -> none  [shifted(): return lax.ppermute(block, axis, route)]
    while x4 -> x0, local copies, waits for them, and re-layouts: 5.01 us -> none  [the longest x1 4.75 us: shards(): lax.scan(advance, running_start, jnp.arange(micro_count + sections - 1))]
    ppermute x3 -> x0, starting transfers between devices: 3.88 us -> none  [shifted(): return lax.ppermute(block, axis, route)]
  transfers between devices with their start and end apart: 12 -> 0, of which waited for: 6 -> 0; matrix products, arithmetic and copies ran while one was open for 3% -> 0% of each run, Pallas kernels for 0% -> 0%
where the time goes in v1:
time: 107 us
  Pallas kernels  100 us (93%)
  local copies, waits for them, and re-layouts  6.16 us (6%)
    pallas_call x1, Pallas kernels, shards(): pl.pallas_call(functools.partial(kernel, sections, dps, towers), out_shap...  100 us
    unnamed x11, local copies, waits for them, and re-layouts  6.16 us

profile of v1, /device:TPU:5, one launch (start us, length us, event | category | flops | bytes accessed | tf_op | source)
XLA Modules:
  0.0 106.6 jit_solution(6120231768404399922)
XLA Ops:
  0.0 0.0 copy-start
  0.0 1.9 %copy-done = bf16[1,1,4096,1,3,128]{5,2,4,3,1,0:T(8,128)(2,1)S(1)} copy-done((bf16[1,1,4096,1,3,128]{5,2,4,3,1,0:T(8,128)(2,1)S(1)}, bf16[1,1,4096,1,3,128]{5,2,4,3,1,0:T(8,128)(2,1)}, u32[]{:S(2)}) %copy-start) | copy-done | bytes 3145752
  1.9 0.0 copy-start.1
  1.9 1.2 %copy-done.1 = bf16[1,1,4,128,1024]{4,3,2,1,0:T(8,128)(2,1)S(1)} copy-done((bf16[1,1,4,128,1024]{4,3,2,1,0:T(8,128)(2,1)S(1)}, bf16[1,1,4,128,1024]{4,3,2,1,0:T(8,128)(2,1)}, u32[]{:S(2)}) %copy-start.1) | copy-done | bytes 1048600
  3.1 0.0 copy-start.2
  3.1 0.9 copy-done.2
  4.1 0.0 copy-start.3
  4.1 0.7 copy-done.3
  4.8 0.0 copy-start.4
  4.8 0.7 copy-done.4
  5.5 100.5 %relay.1 = bf16[1,2,64,1024]{3,2,1,0:T(8,128)(2,1)S(1)} custom-call(bf16[2,64,1024]{2,1,0:T(8,128)(2,1)S(1)} %copy-done.2, s32[2,1,64]{2,1,0:T(1,128)S(1)} %bitcast.11, f32[1,4096]{1,0:T(1,128)S(1)} %bitcast.10, bf16[3,4096,128]{2,1,0:T(8,128)(2,1)S(1)} %bitcast.8, bf16[512,1024]{1,0:T(8,128)(2,1)S(1)} %bitcast.9), custom_call_target="tpu_custom_call" | custom-call | tf_op jit(solution)/shard_map/relay/pallas_call | solution.py:296
  105.9 0.7 copy.8
Async XLA Ops:
  0.0 1.9 %copy-start = (bf16[1,1,4096,1,3,128]{5,2,4,3,1,0:T(8,128)(2,1)S(1)}, bf16[1,1,4096,1,3,128]{5,2,4,3,1,0:T(8,128)(2,1)}, u32[]{:S(2)}) copy-start(bf16[1,1,4096,1,3,128]{5,2,4,3,1,0:T(8,128)(2,1)} %param.8) | copy-start | bytes 9437188
  1.9 1.2 %copy-start.1 = (bf16[1,1,4,128,1024]{4,3,2,1,0:T(8,128)(2,1)S(1)}, bf16[1,1,4,128,1024]{4,3,2,1,0:T(8,128)(2,1)}, u32[]{:S(2)}) copy-start(bf16[1,1,4,128,1024]{4,3,2,1,0:T(8,128)(2,1)} %param.9) | copy-start | bytes 3145732
  3.1 0.9 copy-start.2
  4.1 0.7 copy-start.3
  4.8 0.7 copy-start.4

commit v2 on v1

--- a/solution.py
+++ b/solution.py
@@ -20,9 +20,9 @@
 
 def kernel(
     sections, dps, towers,
-    stream, routes, gain, qkv_hbm, out_hbm, out,
-    w_in, w_out, routes_of, spread_of, rows_in, shares, outbound, inbound,
-    queries, kv_out, kv_all, heads, updated, returned,
+    stream, routes, gain_hbm, qkv_hbm, out_hbm, out,
+    w_in, w_out, gain, routes_in, routes_of, spread_of, shares, outbound, inbound,
+    total, squares, queries, kv_out, kv_all, heads, updated, returned,
     w_sem, r_send, r_recv, z_send, z_recv, x_send, x_recv, kv_send, kv_recv,
     a_send, a_recv, b_send, b_recv, s_send, s_recv,
 ):
@@ -30,6 +30,8 @@
     slots = rows // 2
     routed = towers * slots
     head = qkv_hbm.shape[2]
+    part = shares.shape[3]
+    parts = width // part
     section_at = lax.axis_index("section")
     dp_at = lax.axis_index("dp")
     tower_at = lax.axis_index("tower")
@@ -46,6 +48,22 @@
         for j in range(3)
     ]
     weight_copies.append(pltpu.make_async_copy(out_hbm, w_out, w_sem.at[3]))
+    weight_copies.append(pltpu.make_async_copy(gain_hbm, gain, w_sem.at[4]))
+    routes_copy = pltpu.make_async_copy(routes, routes_in, w_sem.at[5])
+    routes_copy.start()
+    stream_copies = [
+        pltpu.make_async_copy(
+            stream.at[u // parts, :, pl.ds(u % parts * part, part)],
+            shares.at[u, dp_at], w_sem.at[6 + u],
+        )
+        for u in range(micros * parts)
+    ]
+
+    @pl.when(section_at == 0)
+    def _():
+        for copy in stream_copies:
+            copy.start()
+
     for copy in weight_copies:
         copy.start()
 
@@ -65,8 +83,9 @@
             barrier, inc=1, device_id={"section": prev_section}, device_id_type=MESH
         )
 
+    routes_copy.wait()
     for m in range(micros):
-        routes_of[tower_at, m : m + 1, 0:rows] = routes[m]
+        routes_of[tower_at, m : m + 1, 0:rows] = routes_in[m]
 
     @pl.when(section_at < sections - 1)
     def _():
@@ -114,58 +133,103 @@
 
     relays = [
         pltpu.make_async_remote_copy(
-            src_ref=out.at[0, m], dst_ref=rows_in.at[m], send_sem=s_send.at[m],
-            recv_sem=s_recv.at[m], device_id={"section": next_section}, device_id_type=MESH,
-        )
-        for m in range(micros)
+            src_ref=out.at[0, u // parts, :, pl.ds(u % parts * part, part)],
+            dst_ref=shares.at[u, dp_at], send_sem=s_send.at[u],
+            recv_sem=s_recv.at[u], device_id={"section": next_section}, device_id_type=MESH,
+        )
+        for u in range(micros * parts)
     ]
-    z_copies, x_copies, kv_copies, a_copies, b_copies = {}, {}, {}, {}, {}
-
-    def enter(m):
+    kv_copies, a_copies, b_copies = {}, {}, {}
+
+    def pass_on(u, owner, way):
+        return pltpu.make_async_remote_copy(
+            src_ref=shares.at[u, owner], dst_ref=shares.at[u, owner],
+            send_sem=z_send.at[u, way, owner], recv_sem=z_recv.at[u, owner],
+            device_id={"dp": lax.rem(dp_at + (1 if way else dps - 1), dps)}, device_id_type=MESH,
+        )
+
+    def tower_copy(u, owner, j):
+        peer = ahead(tower_at, j, towers)
+        return pltpu.make_async_remote_copy(
+            src_ref=outbound.at[u, owner, peer], dst_ref=inbound.at[u, owner, tower_at],
+            send_sem=x_send.at[u, owner, j], recv_sem=x_recv.at[u, owner, j],
+            device_id={"tower": peer}, device_id_type=MESH,
+        )
+
+    def forward(u, owner, way):
+        @pl.when(dp_at < dps - 1 if way else dp_at > 0)
+        def _():
+            pass_on(u, owner, way).start()
+
+    def begin(m, ready):
+        for u in range(m * parts, (m + 1) * parts):
+            ready(u)
+            if dps > 1:
+                forward(u, dp_at, 0)
+                forward(u, dp_at, 1)
+            route(u, dp_at)
+
+    def enter_first(m):
         @pl.when(section_at == 0)
         def _():
-            rows_in[m] = stream[m]
-
+            begin(m, lambda u: stream_copies[u].wait())
+
+    def enter_later(m):
         @pl.when(section_at > 0)
         def _():
-            relays[m].wait_recv()
-
-        for k in range(1, dps):
-            z_copies[m, k] = send(
-                rows_in.at[m], shares.at[m, k], z_send.at[m, k], z_recv.at[m, k],
-                {"dp": ahead(dp_at, k, dps)},
-            )
-
-    def route(m, k):
-        if k == 0:
-            share = rows_in[m]
+            begin(m, lambda u: relays[u].wait_recv())
+
+    def route(m, owner):
+        spread = spread_of[m // parts, tower_at].reshape(routed, rows)
+        picked = jnp.dot(spread, shares[m, owner], preferred_element_type=jnp.float32)
+        outbound[m, owner] = picked.astype(jnp.bfloat16).reshape(towers, slots, part)
+        for j in range(1, towers):
+            tower_copy(m, owner, j).start()
+        inbound[m, owner, tower_at] = outbound[m, owner, tower_at]
+
+    def both_sides(k, act):
+        @pl.when(dp_at >= k)
+        def _():
+            act(dp_at - k, 1)
+
+        @pl.when(dp_at < dps - k)
+        def _():
+            act(dp_at + k, 0)
+
+    def hop(m, k):
+        for u in range(m * parts, (m + 1) * parts):
+            def act(owner, way):
+                pass_on(u, owner, way).wait_recv()
+                forward(u, owner, way)
+                route(u, owner)
+
+            both_sides(k, act)
+
+    def gather_in(m, owner, first):
+        at = pl.ds(pl.multiple_of(owner * width + m % parts * part, part), part)
+        for j in range(1, towers):
+            tower_copy(m, owner, j).wait_recv()
+        value = inbound[m, owner].reshape(routed, part).astype(jnp.float32)
+        square = jnp.sum(value * value, axis=1, keepdims=True)
+        scaled = (value * gain[:, at]).astype(jnp.bfloat16)
+        made = jnp.dot(scaled, w_in[at, :], preferred_element_type=jnp.float32)
+        if first:
+            squares[...] = jnp.broadcast_to(square, squares.shape)
+            total[...] = made
         else:
-            z_copies[m, k].wait_recv()
-            share = shares[m, k]
-        spread = spread_of[m, tower_at].reshape(routed, rows)
-        picked = jnp.dot(spread, share, preferred_element_type=jnp.float32)
-        outbound[m, k] = picked.astype(jnp.bfloat16).reshape(towers, slots, width)
-        for j in range(1, towers):
-            peer = ahead(tower_at, j, towers)
-            x_copies[m, k, j] = send(
-                outbound.at[m, k, peer], inbound.at[m, k, tower_at],
-                x_send.at[m, k, j], x_recv.at[m, k, j], {"tower": peer},
-            )
-        inbound[m, k, tower_at] = outbound[m, k, tower_at]
+            squares[...] += jnp.broadcast_to(square, squares.shape)
+            total[...] += made
+
+    def collect(m, k):
+        for u in range(m * parts, (m + 1) * parts):
+            if k == 0:
+                gather_in(u, dp_at, u % parts == 0)
+            else:
+                both_sides(k, lambda owner, way: gather_in(u, owner, False))
 
     def project_in(m):
-        total = jnp.zeros((routed, 3 * head), jnp.float32)
-        squares = jnp.zeros((routed, 1), jnp.float32)
-        for k in range(dps):
-            for j in range(1, towers):
-                x_copies[m, k, j].wait_recv()
-            owner = lax.rem(dp_at + dps - k, dps)
-            at = pl.ds(pl.multiple_of(owner * width, width), width)
-            value = inbound[m, k].reshape(routed, width).astype(jnp.float32)
-            squares = squares + jnp.sum(value * value, axis=1, keepdims=True)
-            scaled = (value * gain[:, at]).astype(jnp.bfloat16)
-            total = total + jnp.dot(scaled, w_in[at, :], preferred_element_type=jnp.float32)
-        mixed = total * lax.rsqrt(squares / (width * dps) + NORM_EPSILON)
+        inverse = lax.rsqrt(squares[:, 0:1] / (width * dps) + NORM_EPSILON)
+        mixed = total[...] * inverse
         queries[m] = mixed[:, :head].astype(jnp.bfloat16)
         kv_out[m] = mixed[:, head:].astype(jnp.bfloat16).reshape(towers, slots, 2 * head)
         for j in range(1, towers):
@@ -225,59 +289,90 @@
     def project_out(m):
         for k in range(1, dps):
             a_copies[m, k].wait_recv()
-        made = jnp.dot(heads[m], w_out[...], preferred_element_type=jnp.float32)
-        own = inbound[m, 0].reshape(routed, width).astype(jnp.float32)
-        updated[m] = (own + made).astype(jnp.bfloat16).reshape(towers, slots, width)
-        for j in range(1, towers):
-            peer = ahead(tower_at, j, towers)
-            b_copies[m, j] = send(
-                updated.at[m, peer], returned.at[m, tower_at], b_send.at[m, j], b_recv.at[m, j],
-                {"tower": peer},
+        for c in range(parts):
+            u = m * parts + c
+            made = jnp.dot(
+                heads[m], w_out[:, c * part : (c + 1) * part], preferred_element_type=jnp.float32
             )
-        returned[m, tower_at] = updated[m, tower_at]
+            own = inbound[u, dp_at].reshape(routed, part).astype(jnp.float32)
+            updated[u] = (own + made).astype(jnp.bfloat16).reshape(towers, slots, part)
+            for j in range(1, towers):
+                peer = ahead(tower_at, j, towers)
+                b_copies[u, j] = send(
+                    updated.at[u, peer], returned.at[u, tower_at],
+                    b_send.at[u, j], b_recv.at[u, j], {"tower": peer},
+                )
+            returned[u, tower_at] = updated[u, tower_at]
 
     def leave(m):
-        for j in range(1, towers):
-            b_copies[m, j].wait_recv()
         spread = spread_of[m, tower_at].reshape(routed, rows)
-        out[0, m] = unslot(spread, returned[m].reshape(routed, width)).astype(jnp.bfloat16)
-
-        @pl.when(section_at < sections - 1)
-        def _():
-            relays[m].start()
+        for c in range(parts):
+            u = m * parts + c
+            for j in range(1, towers):
+                b_copies[u, j].wait_recv()
+            moved = unslot(spread, returned[u].reshape(routed, part))
+            out[0, m, :, c * part : (c + 1) * part] = moved.astype(jnp.bfloat16)
+
+            @pl.when(section_at < sections - 1)
+            def _():
+                relays[u].start()
 
     for m in range(micros):
         make_spread(m, tower_at)
-    enter(0)
-    for k in range(dps):
-        route(0, k)
-    for k in range(1, towers):
-        route_copies[k - 1].wait_recv()
-        for m in range(micros):
-            make_spread(m, lax.rem(tower_at + towers - k, towers))
-    for copy in weight_copies:
-        copy.wait()
-
-    later = [project_in, attend, project_out, leave]
+    enter_first(0)
+    enter_later(0)
+    for k in range(1, dps):
+        hop(0, k)
+        if k == 1:
+            for copy in weight_copies:
+                copy.wait()
+            for j in range(1, towers):
+                route_copies[j - 1].wait_recv()
+                for n in range(micros):
+                    make_spread(n, lax.rem(tower_at + towers - j, towers))
+        if k == max(1, dps - 2) and micros > 1:
+            enter_first(1)
+        collect(0, k - 1)
     for m in range(micros):
-        pending = list(range(dps)) if m + 1 < micros else []
-        if pending:
-            enter(m + 1)
-            route(m + 1, pending.pop(0))
-        for number, step in enumerate(later):
-            step(m)
-            left = len(later) - 1 - number
-            if pending and left:
-                for k in range(-(-len(pending) // left)):
-                    route(m + 1, pending.pop(0))
+        collect(m, dps - 1)
+        project_in(m)
+        following = m + 1 < micros
+        if following:
+            enter_later(m + 1)
+            for k in range(1, dps - 1):
+                hop(m + 1, k)
+        attend(m)
+        if following:
+            hop(m + 1, dps - 1)
+        project_out(m)
+        if following:
+            collect(m + 1, 0)
+        leave(m)
+        if following:
+            if m + 2 < micros:
+                enter_first(m + 2)
+            for k in range(1, dps - 1):
+                collect(m + 1, k)
 
     for copy in started:
         copy.wait_send()
+    for u in range(micros * parts):
+        for owner in range(dps):
+            for j in range(1, towers):
+                tower_copy(u, owner, j).wait_send()
+
+            @pl.when((dp_at >= owner) & (dp_at < dps - 1))
+            def _():
+                pass_on(u, owner, 1).wait_send()
+
+            @pl.when((dp_at <= owner) & (dp_at > 0))
+            def _():
+                pass_on(u, owner, 0).wait_send()
 
     @pl.when(section_at < sections - 1)
     def _():
-        for m in range(micros):
-            relays[m].wait_send()
+        for u in range(micros * parts):
+            relays[u].wait_send()
 
 
 def shards(stream, routes, tower_gain, qkv_weight, out_weight):
@@ -289,6 +384,9 @@
     model = tower_gain.shape[-1]
     slots = rows // 2
     routed = towers * slots
+    parts = 2
+    units = micros * parts
+    part = width // parts
     bf16 = jnp.bfloat16
     dma = pltpu.SemaphoreType.DMA
     vmem = pl.BlockSpec(memory_space=pltpu.VMEM)
@@ -296,34 +394,37 @@
     return pl.pallas_call(
         functools.partial(kernel, sections, dps, towers),
         out_shape=jax.ShapeDtypeStruct((1, micros, rows, width), bf16),
-        in_specs=[vmem, vmem, vmem, hbm, hbm],
+        in_specs=[hbm] * 5,
         out_specs=vmem,
         scratch_shapes=[
             pltpu.VMEM((model, 3 * head), bf16),
             pltpu.VMEM((dps * head, width), bf16),
+            pltpu.VMEM((1, model), jnp.float32),
+            pltpu.VMEM((micros, 1, rows), jnp.int32),
             pltpu.VMEM((towers, 8, 128), jnp.int32),
             pltpu.VMEM((micros, towers, towers, slots, rows), bf16),
-            pltpu.VMEM((micros, rows, width), bf16),
-            pltpu.VMEM((micros, dps, rows, width), bf16),
-            pltpu.VMEM((micros, dps, towers, slots, width), bf16),
-            pltpu.VMEM((micros, dps, towers, slots, width), bf16),
+            pltpu.VMEM((units, dps, rows, part), bf16),
+            pltpu.VMEM((units, dps, towers, slots, part), bf16),
+            pltpu.VMEM((units, dps, towers, slots, part), bf16),
+            pltpu.VMEM((routed, 3 * head), jnp.float32),
+            pltpu.VMEM((routed, 128), jnp.float32),
             pltpu.VMEM((micros, routed, head), bf16),
             pltpu.VMEM((micros, towers, slots, 2 * head), bf16),
             pltpu.VMEM((micros, towers, towers, slots, 2 * head), bf16),
             pltpu.VMEM((micros, routed, dps * head), bf16),
-            pltpu.VMEM((micros, towers, slots, width), bf16),
-            pltpu.VMEM((micros, towers, slots, width), bf16),
-            dma((4,)),
+            pltpu.VMEM((units, towers, slots, part), bf16),
+            pltpu.VMEM((units, towers, slots, part), bf16),
+            dma((6 + units,)),
             dma((towers,)), dma((towers,)),
-            dma((micros, dps)), dma((micros, dps)),
-            dma((micros, dps, towers)), dma((micros, dps, towers)),
+            dma((units, 2, dps)), dma((units, dps)),
+            dma((units, dps, towers)), dma((units, dps, towers)),
             dma((micros, towers)), dma((micros, towers)),
             dma((micros, dps)), dma((micros, dps)),
-            dma((micros, towers)), dma((micros, towers)),
-            dma((micros,)), dma((micros,)),
+            dma((units, towers)), dma((units, towers)),
+            dma((units,)), dma((units,)),
         ],
         compiler_params=pltpu.CompilerParams(
-            collective_id=0, has_side_effects=True, vmem_limit_bytes=48 * 1024 * 1024
+            collective_id=0, has_side_effects=True, vmem_limit_bytes=60 * 1024 * 1024
         ),
         name="relay",
     )(

time: 107 us -> 93.4 us (0.87)
  Pallas kernels: 100 us -> 90.7 us
  local copies, waits for them, and re-layouts: 6.16 us -> 1.67 us
    pallas_call x1, Pallas kernels: 100 us -> 90.7 us  [shards(): pl.pallas_call(functools.partial(kernel, sections, dps, towers), out_shap...]
    unnamed x11 -> x1, local copies, waits for them, and re-layouts: 6.16 us -> 1.67 us
where the time goes in v2:
time: 93.4 us; the launch traced here: 92.4 us
  Pallas kernels  90.7 us (97%)
  local copies, waits for them, and re-layouts  1.67 us (2%)
    pallas_call x1, Pallas kernels, shards(): pl.pallas_call(functools.partial(kernel, sections, dps, towers), out_shap...  90.7 us

profile of v2, /device:TPU:5, one launch (start us, length us, event | category | flops | bytes accessed | tf_op | source)
XLA Modules:
  0.0 92.4 jit_solution(16428227483864558750)
XLA Ops:
  0.0 90.7 %relay.1 = bf16[1,2,64,1024]{3,2,1,0:T(8,128)(2,1)} custom-call(bf16[2,64,1024]{2,1,0:T(8,128)(2,1)} %stream.1, s32[2,1,64]{2,1,0:T(1,128)} %bitcast.11, f32[1,4096]{1,0:T(1,128)} %bitcast.10, bf16[3,4096,128]{2,1,0:T(8,128)(2,1)} %bitcast.8, bf16[512,1024]{1,0:T(8,128)(2,1)} %bitcast.9), custom_call_target="tpu_custom_call" | custom-call | tf_op jit(solution)/shard_map/relay/pallas_call | solution.py:394
  90.7 1.7 %copy.8 = bf16[1,2,64,1024]{3,2,1,0:T(8,128)(2,1)} copy(bf16[1,2,64,1024]{3,2,1,0:T(8,128)(2,1)} %relay.1) | data formatting | bytes 524288

commit v3 on v2

--- a/solution.py
+++ b/solution.py
@@ -339,20 +339,20 @@
         following = m + 1 < micros
         if following:
             enter_later(m + 1)
+        attend(m)
+        if following:
             for k in range(1, dps - 1):
                 hop(m + 1, k)
-        attend(m)
-        if following:
-            hop(m + 1, dps - 1)
         project_out(m)
         if following:
-            collect(m + 1, 0)
+            for k in range(dps - 1, dps):
+                hop(m + 1, k)
+        if following:
+            for k in range(0, dps - 1):
+                collect(m + 1, k)
         leave(m)
-        if following:
-            if m + 2 < micros:
-                enter_first(m + 2)
-            for k in range(1, dps - 1):
-                collect(m + 1, k)
+        if following and m + 2 < micros:
+            enter_first(m + 2)
 
     for copy in started:
         copy.wait_send()

time: 93.4 us -> 92.3 us (0.988)
  no operation moved by 1% of the time
where the time goes in v3:
time: 92.3 us; the launch traced here: 91.6 us
  Pallas kernels  90 us (98%)
  local copies, waits for them, and re-layouts  1.67 us (2%)
    pallas_call x1, Pallas kernels, shards(): pl.pallas_call(functools.partial(kernel, sections, dps, towers), out_shap...  90 us

profile of v3, /device:TPU:5, one launch (start us, length us, event | category | flops | bytes accessed | tf_op | source)
XLA Modules:
  0.0 91.6 jit_solution(18404664224013369659)
XLA Ops:
  0.0 90.0 %relay.1 = bf16[1,2,64,1024]{3,2,1,0:T(8,128)(2,1)} custom-call(bf16[2,64,1024]{2,1,0:T(8,128)(2,1)} %stream.1, s32[2,1,64]{2,1,0:T(1,128)} %bitcast.11, f32[1,4096]{1,0:T(1,128)} %bitcast.10, bf16[3,4096,128]{2,1,0:T(8,128)(2,1)} %bitcast.8, bf16[512,1024]{1,0:T(8,128)(2,1)} %bitcast.9), custom_call_target="tpu_custom_call" | custom-call | tf_op jit(solution)/shard_map/relay/pallas_call | solution.py:394
  90.0 1.7 %copy.8 = bf16[1,2,64,1024]{3,2,1,0:T(8,128)(2,1)} copy(bf16[1,2,64,1024]{3,2,1,0:T(8,128)(2,1)} %relay.1) | data formatting | bytes 524288
